TPU v7x, 256 devices: a whole 4x4x8 slice. The times are simulated.
256 devices in a mesh: blk: 128 (over y_hi, x, z, core), sub: 2 (over y_lo).
Axes of the slice: x: 4, y: 4 (y_hi: 2, y_lo: 2; y = y_hi * 2 + y_lo), z: 8, core: 2. Of those that a mesh axis runs over, the one named last changes fastest.
Arguments:
- adjoint_start: float32 [5, 4096, 16, 128], P(None, 'blk', 'sub'), may hold values from -6 to 6
- objective_grad: float32 [5, 4096, 16, 128], P(None, 'blk', 'sub'), may hold values from -6 to 6
- flux_jacobian: bfloat16 [3, 5, 5, 4096, 16, 128], P(None, None, None, 'blk', 'sub'), may hold values from -3 to 3
- stab_block: bfloat16 [5, 5, 4096, 16, 128], P(None, None, 'blk', 'sub'), as said below
- precond_block: bfloat16 [5, 5, 4096, 16, 128], P(None, None, 'blk', 'sub'), as said below
- wall_weight: float32 [5, 2], replicated, may hold values from -4 to 4
- wall_geometry: bfloat16 [524288, 2, 128], P('blk'), may hold values from -6 to 6
- face_patch: int32 [524288], P('blk'), may hold values from 0 to 2047
- patch_slot: int32 [2048], replicated, may hold values from 0 to 2047, each once
Outputs:
- adjoint_state: float32 [5, 4096, 16, 128], P(None, 'blk', 'sub')
- patch_sens: float32 [2048, 128], P('blk')
Inputs may be any that keep to these rules, and one draw needn't show every extreme that they name: `stab_block`: diagonal entries between 2 and 4, off-diagonal ones smaller in magnitude than 2. `precond_block`: diagonal entries between 0.15 and 0.3, off-diagonal ones smaller in magnitude than 0.15.
All inputs are finite; a program needn't handle non-finite values.
Results may differ from a plain program's by a relative error of at most 0.0003.
Values sent between devices are 32-bit elements; how exact they have to be, the bound alone decides.
A program may use at most 128 MiB of HBM per device.

v0:
```python
import jax
import jax.numpy as jnp
from jax import lax
from jax.sharding import PartitionSpec as P


def padded_2(array, sides, width):
    for axis, dim in sides:
        peers, length = (lax.axis_size(axis), array.shape[dim])
        up = [(i, (i + 1) % peers) for i in range(peers - 1)]
        down = [(j, i) for i, j in up]
        last = lax.slice_in_dim(array, length - width, length, axis=dim)
        leading = lax.slice_in_dim(array, 0, width, axis=dim)
        before = lax.ppermute(last, axis, up)
        after = lax.ppermute(leading, axis, down)
        array = jnp.concatenate([before, array, after], axis=dim)
    return array


def transposed(matrix, field):
    return jnp.sum(matrix * field[:, None], axis=0)


def sweep(state, flux_jacobian, stab_block, precond_block, objective_grad):
    grown = padded_2(state, (("blk", 1), ("sub", 2)), 1)
    padded = jnp.pad(grown, ((0, 0), (0, 0), (0, 0), (1, 1)))
    diff_a = padded[:, :-2, 1:-1, 1:-1] - padded[:, 2:, 1:-1, 1:-1]
    diff_n = padded[:, 1:-1, :-2, 1:-1] - padded[:, 1:-1, 2:, 1:-1]
    diff_c = padded[:, 1:-1, 1:-1, :-2] - padded[:, 1:-1, 1:-1, 2:]
    jac = flux_jacobian.astype(jnp.float32)
    resid = objective_grad - transposed(stab_block.astype(jnp.float32), state)
    resid = resid - 0.5 * (
        transposed(jac[0], diff_a) + transposed(jac[1], diff_n) + transposed(jac[2], diff_c)
    )
    return state + jnp.sum(precond_block.astype(jnp.float32) * resid[None, :], axis=1)


def patch_partial(wall_psi, wall_weight, geometry_rows, patch_rows, patch_slot, weight_mask):
    sens_p = jnp.sum(wall_weight[:, 0:1] * wall_psi, axis=0)
    sens_t = jnp.sum(wall_weight[:, 1:2] * wall_psi, axis=0)
    geometry = geometry_rows.astype(jnp.float32)
    contribution = (
        sens_p[:, None] * geometry[:, 0, :] + sens_t[:, None] * geometry[:, 1, :]
    ) * weight_mask
    slots = patch_slot[patch_rows]
    return jax.ops.segment_sum(contribution, slots, num_segments=patch_slot.shape[0])


def local(
    adjoint_start,
    objective_grad,
    flux_jacobian,
    stab_block,
    precond_block,
    wall_weight,
    wall_geometry,
    face_patch,
    patch_slot,
):
    state = adjoint_start
    for index in range(2):
        state = sweep(state, flux_jacobian, stab_block, precond_block, objective_grad)
    block_odd = lax.axis_index("blk") % 2
    wall_device = block_odd * (lax.axis_size("sub") - 1)
    wall_cells = jnp.where(block_odd == 1, state[:, :, state.shape[2] - 1, :], state[:, :, 0, :])
    wall_psi = wall_cells.reshape(state.shape[0], -1)
    at_wall = (lax.axis_index("sub") == wall_device).astype(jnp.float32)
    partial_sums = patch_partial(
        wall_psi, wall_weight, wall_geometry, face_patch, patch_slot, at_wall
    )
    paired = lax.psum(partial_sums, "sub")
    patch_sens = lax.psum_scatter(paired, "blk", scatter_dimension=0, tiled=True)
    return (state, patch_sens)


def solution(mesh):
    return jax.shard_map(
        local,
        mesh=mesh,
        in_specs=(
            P(None, "blk", "sub", None),
            P(None, "blk", "sub", None),
            P(None, None, None, "blk", "sub", None),
            P(None, None, "blk", "sub", None),
            P(None, None, "blk", "sub", None),
            P(),
            P("blk", None, None),
            P("blk"),
            P(),
        ),
        out_specs=(P(None, "blk", "sub", None), P("blk", None)),
        check_vma=False,
    )
```

profile of v0, /device:TPU:1, one launch (start us, length us, event | category | flops | bytes accessed | tf_op | source)
XLA Modules:
  0.0 779.8 jit_solution(2723968023582265073)
XLA Ops:
  7.2 0.0 copy-start
  7.2 0.0 reduce-scatter.2.cloned.1.call-start
  7.2 0.9 fusion.22
  8.1 4.9 collective-permute-start
  13.1 1.9 collective-permute-start.1
  15.0 0.0 slice-start
  15.0 2.2 fusion.2
  17.2 0.0 copy-done.3
  17.2 0.0 copy-start.10
  17.2 0.0 copy-start.2
  17.2 0.0 slice-start.1
  17.2 4.1 fusion.20
  21.4 0.1 copy.31
  21.5 0.0 slice-done
  21.5 0.0 slice-done.1
  21.5 1.3 convert_element_type.23
  22.9 0.0 copy-start.1
  22.9 0.0 collective-permute-done
  22.9 0.0 collective-permute-done.1
  22.9 3.2 collective-permute-start.2
  26.1 1.3 collective-permute-start.3
  27.5 0.3 collective-permute-done.2
  27.8 3.7 collective-permute-done.3
  31.5 0.8 select_maximum_fusion.4
  32.3 0.3 slice_subtract_fusion.1
  32.6 0.4 copy.33
  33.0 0.1 fusion.16
  33.1 0.4 copy.32
  33.5 0.0 copy-start.8
  33.5 1.4 multiply_reduce_fusion.4
  34.9 0.0 copy-start.6
  34.9 0.2 multiply_subtract_fusion.1
  35.1 1.2 copy-done.6
  36.3 0.3 fusion
  36.6 0.1 add.43
  36.7 5.2 collective-permute-start.4
  41.9 1.9 collective-permute-start.5
  43.9 0.0 copy-start.5
  43.9 23.0 %gather_fusion = s32[4096]{0:T(1024)S(1)} fusion(s32[2048]{0:T(1024)S(1)} %copy-done, s32[4096]{0:T(1024)S(1)} %fusion.19), kind=kCustom, calls=%fused_computation | custom fusion | bytes 49152 | tf_op jit(solution)/shard_map/gather | solution.py:45
  67.0 0.0 collective-permute-done.4
  67.0 0.0 collective-permute-done.5
  67.0 0.1 pad_maximum_fusion.21
  67.1 1.3 collective-permute-start.6
  68.5 1.5 collective-permute-start.7
  69.9 0.3 fusion.3
  70.3 0.0 collective-permute-done.6
  70.3 0.1 copy.35
  70.4 3.5 collective-permute-done.7
  73.9 0.1 copy.37
  74.0 1.5 select_maximum_fusion
  75.5 0.5 fusion.15
  75.9 5.5 multiply_reduce_fusion.1
  81.4 0.0 copy-start.7
  81.4 0.2 multiply_subtract_fusion
  81.6 1.2 copy-done.7
  82.8 0.3 fusion.1
  83.2 0.1 add.46
  83.3 0.0 copy-start.9
  83.3 0.3 multiply_reduce_fusion.7
  83.6 1.1 copy-done.4
  84.7 23.9 %scatter_custom_fusion = f32[2048,128]{1,0:T(8,128)} fusion(s32[4096]{0:T(1024)S(1)} %gather_fusion, f32[4096,128]{1,0:T(8,128)} %bitcast.33, f32[4096,128]{1,0:T(8,128)S(1)} %bitcast.32, f32[]{:T(128)S(6)} %convert_element_type.25, f32[4096]{0:T(1024)S(1)} %bitcast.39, f32[4096]{0:T(1024)S(1)} %bitcast.38, f32[]{:T(128)} %constant.11.clone.1), kind=kCustom, calls=%fused_computation.28 | custom fusion | flops 2621440 | bytes 5275656 | tf_op jit(solution)/shard_map/scatter-add | solution.py:46
  108.6 0.0 reduce-scatter.2.cloned.1.call-update
  108.6 659.4 %reduce-scatter.2.cloned.1.call-done = f32[16,128]{1,0:T(8,128)} async-done(((f32[2048,128]{1,0:T(8,128)}), f32[16,128]{1,0:T(8,128)}) %reduce-scatter.2.cloned.1.call-update) | async-done | bytes 8208 | tf_op jit(solution)/shard_map/reduce_scatter | solution.py:72
  768.0 4.9 psum.8
  (19 shorter events, 0.1 us)
Async XLA Ops:
  7.2 36.8 %copy-start = (s32[2048]{0:T(1024)S(1)}, s32[2048]{0:T(1024)}, u32[]{:S(2)}) copy-start(s32[2048]{0:T(1024)} %param.17) | copy-start | bytes 24580
  7.2 10.0 %copy-start.3 = (bf16[4096,2,128]{2,1,0:T(2,128)(2,1)S(1)}, bf16[4096,2,128]{2,1,0:T(2,128)(2,1)}, u32[]{:S(2)}) copy-start(bf16[4096,2,128]{2,1,0:T(2,128)(2,1)} %param.15) | copy-start | bytes 6291460
  7.2 760.8 %reduce-scatter.2.cloned.1.call-start = ((), (), s32[]{:S(2)}) async-start(), calls=%async_computation.1 | async-start | bytes 1056768 | tf_op jit(solution)/shard_map/reduce_scatter | solution.py:72
  8.1 14.7 %collective-permute-start = (f32[5,1,8,128]{3,1,2,0:T(1,128)S(1)}, f32[5,1,8,128]{3,1,2,0:T(1,128)S(1)}, u32[]{:S(2)}, u32[]{:S(2)}) collective-permute-start(f32[5,1,8,128]{3,1,2,0:T(1,128)S(1)} %bitcast.41), channel_id=1, source_target_pairs={{0,2},{2,4},{4,6},{6,8},{8,10},{10,12},{12,14},{14,16},{16,18},{18... | collective-permute-start | bytes 61448 | tf_op jit(solution)/shard_map/ppermute | solution.py:14
  13.1 9.8 %collective-permute-start.1 = (f32[5,1,8,128]{3,1,2,0:T(1,128)S(1)}, f32[5,1,8,128]{3,1,2,0:T(1,128)S(1)}, u32[]{:S(2)}, u32[]{:S(2)}) collective-permute-start(f32[5,1,8,128]{3,1,2,0:T(1,128)S(1)} %bitcast.40), channel_id=1, source_target_pairs={{2,0},{4,2},{6,4},{8,6},{10,8},{12,10},{14,12},{16,14},{18,16},{20... | collective-permute-start | bytes 61448 | tf_op jit(solution)/shard_map/ppermute | solution.py:15
  15.0 6.5 slice-start
  17.2 4.2 copy-start.10
  17.2 4.2 copy-start.2
  17.2 4.3 slice-start.1
  22.9 10.6 %copy-start.1 = (f32[3,5,5,32,8,128]{5,4,3,2,1,0:T(8,128)}, f32[3,5,5,32,8,128]{5,4,3,2,1,0:T(8,128)S(1)}, u32[]{:S(2)}) copy-start(f32[3,5,5,32,8,128]{5,4,3,2,1,0:T(8,128)S(1)} %convert_element_type.23) | copy-start | bytes 29491204
  22.9 4.9 collective-permute-start.2
  26.1 5.4 collective-permute-start.3
  33.5 1.4 copy-start.8
  34.9 1.4 copy-start.6
  36.3 7.6 copy-start.11
  36.7 30.3 %collective-permute-start.4 = (f32[5,1,8,128]{3,2,1,0:T(8,128)S(1)}, f32[5,1,8,128]{3,2,1,0:T(8,128)S(1)}, u32[]{:S(2)}, u32[]{:S(2)}) collective-permute-start(f32[5,1,8,128]{3,2,1,0:T(8,128)S(1)} %get-tuple-element.20), channel_id=1, source_target_pairs={{0,2},{2,4},{4,6},{6,8},{8,10},{10,12},{12,14},{14,16},{16,18},{18... | collective-permute-start | bytes 61448 | tf_op jit(solution)/shard_map/ppermute | solution.py:14
  41.9 25.0 %collective-permute-start.5 = (f32[5,1,8,128]{3,2,1,0:T(8,128)S(1)}, f32[5,1,8,128]{3,2,1,0:T(8,128)S(1)}, u32[]{:S(2)}, u32[]{:S(2)}) collective-permute-start(f32[5,1,8,128]{3,2,1,0:T(8,128)S(1)} %get-tuple-element.21), channel_id=1, source_target_pairs={{2,0},{4,2},{6,4},{8,6},{10,8},{12,10},{14,12},{16,14},{18,16},{20... | collective-permute-start | bytes 61448 | tf_op jit(solution)/shard_map/ppermute | solution.py:15
  43.9 26.0 %copy-start.5 = (bf16[5,5,32,8,128]{4,3,2,1,0:T(8,128)(2,1)S(1)}, bf16[5,5,32,8,128]{4,3,2,1,0:T(8,128)(2,1)}, u32[]{:S(2)}) copy-start(bf16[5,5,32,8,128]{4,3,2,1,0:T(8,128)(2,1)} %param.12) | copy-start | bytes 4915204
  67.1 3.2 collective-permute-start.6
  68.5 5.4 collective-permute-start.7
  81.4 1.4 copy-start.7
  82.8 1.8 copy-start.4
  83.3 25.3 %copy-start.9 = (f32[5,32,8,128]{3,2,1,0:T(8,128)}, f32[5,32,8,128]{3,2,1,0:T(8,128)S(1)}, u32[]{:S(2)}) copy-start(f32[5,32,8,128]{3,2,1,0:T(8,128)S(1)} %add.46) | copy-start | bytes 1966084
Sparse Core Ops, SparseCore 0:
  108.7 659.2 reduce-scatter.1
where the time goes:
time: 787 us; the launch traced here: 780 us
  waiting for transfers between devices  667 us (85%)
  other arithmetic  39.4 us (5%)
  local copies, waits for them, and re-layouts  32.7 us (4%)
  starting transfers between devices  21.3 us (3%)
  between operations  14.5 us (2%)
    reduce_scatter x1, waiting for transfers between devices, local(): lax.psum_scatter(paired, 'blk', scatter_dimension=0, tiled=True)  659 us
    scatter-add x1, other arithmetic, patch_partial(): jax.ops.segment_sum(contribution, slots, num_segments=patch_slot.shape[0])  23.9 us
    gather x1, local copies, waits for them, and re-layouts, patch_partial(): slots = patch_slot[patch_rows]  23 us
  transfers between devices with their start and end apart: 9, of which 4 were waited for; matrix products, arithmetic and copies ran while one was open for 4% of the time, Pallas kernels for 0%

commit v1 on v0

v1 whole, which is shorter than its diff:
```python
import functools

import jax
import jax.numpy as jnp
from jax import lax
from jax.experimental import pallas as pl
from jax.experimental.pallas import tpu as pltpu
from jax.sharding import PartitionSpec as P

MESH = pl.DeviceIdType.MESH
F32 = jnp.float32
BF16 = jnp.bfloat16

NV = 5
NX, NZ = 4, 8


def kernel(
    start_h, grad_h, jac_h, stab_h, prec_h, weight_s, geom_h, face_v, slot_v,
    state_h, patch_v,
    psi0, psi1, psi2, grad, jac, stab, prec, geom, geom32, onehot, key, contrib, acc,
    nsend0, nrecv0, nsend1, nrecv1, sens_loc, sens,
    core_in, x_out, x_in, z_out, z_in, y_out, y_in,
    load_sem, out_sem, a_send, a_recv, n_send, n_recv, s_send, s_recv,
    c_send, c_recv, x_send, x_recv, z_send, z_recv, y_send, y_recv,
):
    blk, sub = lax.axis_index("blk"), lax.axis_index("sub")
    n_blk = lax.axis_size("blk")
    core = lax.rem(blk, 2)
    z = lax.rem(blk // 2, NZ)
    x = lax.rem(blk // (2 * NZ), NX)
    yh = blk // (2 * NZ * NX)

    def at(yh_, x_, z_, core_):
        return ((yh_ * NX + x_) * NZ + z_) * 2 + core_

    core_peer = (at(yh, x, z, 1 - core), sub)
    x_peer = [(at(yh, lax.rem(x + d, NX), z, core), sub) for d in range(NX)]
    z_peer = [(at(yh, x, lax.rem(z + d, NZ), core), sub) for d in range(NZ)]
    y_peer = [(at(1 - yh, x, z, core), sub), (at(1 - yh, x, z, core), 1 - sub), (blk, 1 - sub)]
    partner = (blk, 1 - sub)
    has_left, has_right = blk > 0, blk < n_blk - 1
    other = jnp.where(core == 1, blk + 1, blk - 1)
    has_other = jnp.logical_and(other >= 0, other < n_blk)

    loads = [
        pltpu.make_async_copy(start_h, psi0.at[:, 8:264, :], load_sem.at[0]),
        pltpu.make_async_copy(geom_h, geom, load_sem.at[1]),
        pltpu.make_async_copy(grad_h, grad, load_sem.at[2]),
        pltpu.make_async_copy(jac_h.at[0:25], jac.at[0:25], load_sem.at[3]),
        pltpu.make_async_copy(jac_h.at[25:50], jac.at[25:50], load_sem.at[4]),
        pltpu.make_async_copy(jac_h.at[50:75], jac.at[50:75], load_sem.at[5]),
        pltpu.make_async_copy(stab_h, stab, load_sem.at[6]),
        pltpu.make_async_copy(prec_h, prec, load_sem.at[7]),
    ]
    for load in loads:
        load.start()

    barrier = pltpu.get_barrier_semaphore()
    peers = [core_peer] + x_peer[1:] + z_peer[1:] + y_peer
    for peer in peers:
        pl.semaphore_signal(barrier, inc=1, device_id=peer, device_id_type=MESH)

    @pl.when(has_other)
    def _():
        pl.semaphore_signal(barrier, inc=1, device_id=(other, sub), device_id_type=MESH)

    zero_plane = jnp.zeros((NV, 8, 128), F32)
    for buf in (psi0, psi1):
        @pl.when(jnp.logical_not(has_left))
        def _():
            buf[:, 0:8, :] = zero_plane

        @pl.when(jnp.logical_not(has_right))
        def _():
            buf[:, 264:272, :] = zero_plane

    loads[0].wait()

    def edge_row(plane):
        return jnp.where(sub == 0, plane[7:8], plane[0:1])

    def pick0(a, carry):
        for v in range(NV):
            nsend0[v, a] = edge_row(psi0[v, pl.ds(pl.multiple_of(8 * a + 8, 8), 8), :])
        return carry

    lax.fori_loop(0, 32, pick0, 0)

    pl.semaphore_wait(barrier, len(peers) + has_other.astype(jnp.int32))

    def a_copies(buf, base):
        right = pltpu.make_async_remote_copy(
            src_ref=buf.at[:, 256:264, :], dst_ref=buf.at[:, 0:8, :],
            send_sem=a_send.at[base], recv_sem=a_recv.at[base],
            device_id=(jnp.minimum(blk + 1, n_blk - 1), sub), device_id_type=MESH)
        left = pltpu.make_async_remote_copy(
            src_ref=buf.at[:, 8:16, :], dst_ref=buf.at[:, 264:272, :],
            send_sem=a_send.at[base + 1], recv_sem=a_recv.at[base + 1],
            device_id=(jnp.maximum(blk - 1, 0), sub), device_id_type=MESH)
        return right, left

    def start_a(buf, base):
        right, left = a_copies(buf, base)

        @pl.when(has_right)
        def _():
            right.start()

        @pl.when(has_left)
        def _():
            left.start()

    def wait_a_recv(buf, base):
        right, left = a_copies(buf, base)

        @pl.when(has_left)
        def _():
            right.wait_recv()

        @pl.when(has_right)
        def _():
            left.wait_recv()

    def wait_a_send(buf, base):
        right, left = a_copies(buf, base)

        @pl.when(has_right)
        def _():
            right.wait_send()

        @pl.when(has_left)
        def _():
            left.wait_send()

    n_copy0 = pltpu.make_async_remote_copy(
        src_ref=nsend0, dst_ref=nrecv0, send_sem=n_send.at[4], recv_sem=n_recv.at[4],
        device_id=partner, device_id_type=MESH)
    n_copy0.start()
    start_a(psi0, 0)

    table = slot_v[...]
    for g in range(4):
        patch = face_v[8 * g:8 * g + 8, :]
        lane, high = patch & 127, patch >> 7
        found = jnp.zeros((8, 128), jnp.int32)
        for j in range(16):
            line = jnp.broadcast_to(table[j:j + 1, :], (8, 128))
            found = jnp.where(high == j, jnp.take_along_axis(line, lane, axis=1), found)
        j_, sub_, core_ = found & 7, (found >> 3) & 1, (found >> 4) & 1
        z_, x_, yh_ = (found >> 5) & 7, (found >> 8) & 3, (found >> 10) & 1
        row = (core_ << 9) + (x_ << 7) + (z_ << 4) + (yh_ << 3) + j_
        key[8 * g:8 * g + 8, :] = jnp.where(sub_ == sub, row, -1)

    def fill(i, carry):
        a = lax.rem(i + 6, 32)
        k = jnp.broadcast_to(key[pl.ds(a, 1), :], (16, 128))
        base = lax.broadcasted_iota(jnp.int32, (16, 128), 0)
        for m in range(64):
            hit = (base + 16 * m) == k
            onehot[16 * m:16 * m + 16, pl.ds(pl.multiple_of(i * 128, 128), 128)] = jnp.where(hit, 1.0, 0.0).astype(BF16)
        return carry

    lax.fori_loop(0, 32, fill, 0)

    loads[1].wait()

    def widen(a, carry):
        geom32[a] = geom[pl.ds(pl.multiple_of(a * 256, 256), 256), :].astype(F32)
        return carry

    lax.fori_loop(0, 32, widen, 0)

    sub_iota = lax.broadcasted_iota(jnp.int32, (16, 128), 0) & 7
    lane_iota = lax.broadcasted_iota(jnp.int32, (16, 128), 1)
    edge_n = jnp.where(
        sub == 0, jnp.where(sub_iota == 7, -1.0, 0.0), jnp.where(sub_iota == 0, 1.0, 0.0)).astype(F32)

    def sweep_pair(p, buf, halo, halo_row):
        rows = pl.ds(pl.multiple_of(16 * p, 16), 16)
        stab_acc, jac_acc, psi = [None] * NV, [None] * NV, [None] * NV

        def add(total, term):
            return term if total is None else total + term

        for u in range(NV):
            four = buf[u, pl.ds(pl.multiple_of(16 * p, 16), 32), :]
            here = four[8:24]
            psi[u] = here
            d_a = four[0:16] - four[16:32]
            before = jnp.concatenate([pltpu.roll(here[0:8], 1, 0), pltpu.roll(here[8:16], 1, 0)], 0)
            after = jnp.concatenate([pltpu.roll(here[0:8], 7, 0), pltpu.roll(here[8:16], 7, 0)], 0)
            ghost = jnp.concatenate([jnp.broadcast_to(halo[u, halo_row], (8, 128)),
                                     jnp.broadcast_to(halo[u, halo_row + 1], (8, 128))], 0)
            d_n = jnp.where(sub_iota == 0, 0.0, before) - jnp.where(sub_iota == 7, 0.0, after) + edge_n * ghost
            d_c = (jnp.where(lane_iota == 0, 0.0, pltpu.roll(here, 1, 1))
                   - jnp.where(lane_iota == 127, 0.0, pltpu.roll(here, 127, 1)))
            for v in range(NV):
                i = u * NV + v
                stab_acc[v] = add(stab_acc[v], stab[i, rows, :].astype(F32) * here)
                jac_acc[v] = add(jac_acc[v], jac[i, rows, :].astype(F32) * d_a)
                jac_acc[v] = jac_acc[v] + jac[25 + i, rows, :].astype(F32) * d_n
                jac_acc[v] = jac_acc[v] + jac[50 + i, rows, :].astype(F32) * d_c
        resid = [grad[v, rows, :] - stab_acc[v] - 0.5 * jac_acc[v] for v in range(NV)]
        result = []
        for u in range(NV):
            step = None
            for v in range(NV):
                step = add(step, prec[u * NV + v, rows, :].astype(F32) * resid[v])
            result.append(psi[u] + step)
        return result

    for load in loads[2:]:
        load.wait()
    n_copy0.wait_recv()
    wait_a_recv(psi0, 0)

    def n_copy1(k):
        part = pl.ds(pl.multiple_of(8 * k, 8), 8)
        return pltpu.make_async_remote_copy(
            src_ref=nsend1.at[:, part], dst_ref=nrecv1.at[:, part], send_sem=n_send.at[k], recv_sem=n_recv.at[k],
            device_id=partner, device_id_type=MESH)

    def first_part(k, carry):
        def pair(i, carry):
            p = lax.rem(i + 15, 16)
            new = sweep_pair(p, psi0, nrecv0, 2 * p)
            for v in range(NV):
                psi1[v, pl.ds(pl.multiple_of(16 * p + 8, 8), 16), :] = new[v]
                nsend1[v, 2 * i] = edge_row(new[v][0:8])
                nsend1[v, 2 * i + 1] = edge_row(new[v][8:16])
            return carry

        lax.fori_loop(4 * k, 4 * k + 4, pair, 0)
        n_copy1(k).start()

        @pl.when(k == 0)
        def _():
            start_a(psi1, 2)

        return carry

    lax.fori_loop(0, 4, first_part, 0)

    is_wall = core == sub
    not_wall = jnp.logical_not(is_wall)

    def s_copy(k):
        part = pl.ds(pl.multiple_of(8 * k, 8), 8)
        return pltpu.make_async_remote_copy(
            src_ref=sens_loc.at[:, part, :], dst_ref=sens.at[:, part, :], send_sem=s_send.at[k], recv_sem=s_recv.at[k],
            device_id=partner, device_id_type=MESH)

    def wall_row(plane):
        return jnp.where(sub == 0, plane[0:1], plane[7:8])

    def second_part(k, carry):
        n_copy1(lax.rem(k + 1, 4)).wait_recv()

        @pl.when(k == 3)
        def _():
            wait_a_recv(psi1, 2)

        def pair(i, carry):
            p = lax.rem(i + 3, 16)
            new = sweep_pair(p, psi1, nrecv1, 2 * lax.rem(i + 4, 16))
            for v in range(NV):
                psi2[v, pl.ds(pl.multiple_of(16 * p, 16), 16), :] = new[v]
            for j in range(2):
                total = weight_s[0, j] * new[0]
                for v in range(1, NV):
                    total = total + weight_s[v, j] * new[v]
                sens_loc[j, pl.ds(2 * i, 1), :] = wall_row(total[0:8])
                sens_loc[j, pl.ds(2 * i + 1, 1), :] = wall_row(total[8:16])
            return carry

        lax.fori_loop(4 * k, 4 * k + 4, pair, 0)

        @pl.when(is_wall)
        def _():
            s_copy(k).start()
            part = pl.ds(pl.multiple_of(8 * k, 8), 8)
            sens[:, part, :] = sens_loc[:, part, :]

        return carry

    lax.fori_loop(0, 4, second_part, 0)
    state_copy = pltpu.make_async_copy(psi2, state_h, out_sem)
    state_copy.start()

    def make_contrib(k):
        @pl.when(not_wall)
        def _():
            s_copy(k).wait_recv()

        part = pl.ds(pl.multiple_of(8 * k, 8), 8)
        pressure = jnp.transpose(sens[0, part, :])
        shear = jnp.transpose(sens[1, part, :])
        for r in range(8):
            a = lax.rem(8 * k + 6 + r, 32)
            g0 = geom32[a, pl.ds(0, 128, 2), :]
            g1 = geom32[a, pl.ds(1, 128, 2), :]
            c = pressure[:, r:r + 1] * g0 + shear[:, r:r + 1] * g1
            hi = c.astype(BF16)
            lo = (c - hi.astype(F32)).astype(BF16)
            contrib[128 * r:128 * r + 128, 0:128] = hi
            contrib[128 * r:128 * r + 128, 128:256] = lo

    def product(row, k):
        part = onehot[pl.ds(pl.multiple_of(row, 128), 128), pl.ds(pl.multiple_of(k * 1024, 1024), 1024)]
        both = jnp.dot(part, contrib[...], preferred_element_type=F32)
        return both[:, 0:128] + both[:, 128:256]

    acc[...] = jnp.zeros((1024, 128), F32)

    def quarter(k, carry):
        make_contrib(k)

        def block(m, carry):
            rows = pl.ds(pl.multiple_of(m * 128, 128), 128)
            acc[rows, :] += product(m * 128, k)
            return carry

        lax.fori_loop(0, 8, block, 0)
        return carry

    lax.fori_loop(0, 3, quarter, 0)
    make_contrib(3)

    def order(k):
        return lax.rem(k + 2, 4)

    def c_copy(k):
        start = (1 - core) * 512 + lax.rem(x + order(k), NX) * 128
        return pltpu.make_async_remote_copy(
            src_ref=acc.at[pl.ds(pl.multiple_of(start, 128), 128), :], dst_ref=core_in.at[k],
            send_sem=c_send.at[k], recv_sem=c_recv.at[k], device_id=core_peer, device_id_type=MESH)

    def x_copy(k):
        peer = (at(yh, lax.rem(x + order(k), NX), z, core), sub)
        return pltpu.make_async_remote_copy(
            src_ref=x_out.at[k], dst_ref=x_in.at[k],
            send_sem=x_send.at[k], recv_sem=x_recv.at[k], device_id=peer, device_id_type=MESH)

    def away(k, carry):
        start = (1 - core) * 512 + lax.rem(x + order(k), NX) * 128
        rows = pl.ds(pl.multiple_of(start, 128), 128)
        acc[rows, :] += product(start, 3)
        c_copy(k).start()
        return carry

    lax.fori_loop(0, 4, away, 0)

    def kept(k, carry):
        start = core * 512 + lax.rem(x + order(k), NX) * 128
        rows = pl.ds(pl.multiple_of(start, 128), 128)
        mine = acc[rows, :] + product(start, 3)
        c_copy(k).wait_recv()
        x_out[k] = mine + core_in[k]

        @pl.when(order(k) != 0)
        def _():
            x_copy(k).start()

        return carry

    lax.fori_loop(0, 4, kept, 0)
    for k in (1, 3, 0):
        x_copy(k).wait_recv()
    z_out[...] = x_out[2] + x_in[0] + x_in[1] + x_in[3]

    def z_copy(d):
        dest = lax.rem(z + d, NZ)
        peer = (at(yh, x, dest, core), sub)
        return pltpu.make_async_remote_copy(
            src_ref=z_out.at[pl.ds(pl.multiple_of(dest * 16, 16), 16), :], dst_ref=z_in.at[d - 1],
            send_sem=z_send.at[d - 1], recv_sem=z_recv.at[d - 1], device_id=peer, device_id_type=MESH)

    for d in (4, 3, 5, 2, 6, 1, 7):
        z_copy(d).start()
    for d in range(1, NZ):
        z_copy(d).wait_recv()
    total = z_out[pl.ds(pl.multiple_of(z * 16, 16), 16), :]
    for d in range(NZ - 1):
        total = total + z_in[d]
    y_out[...] = total

    y_rows = [1 - yh, 1 - yh, yh]

    def y_copy(k):
        return pltpu.make_async_remote_copy(
            src_ref=y_out.at[pl.ds(pl.multiple_of(y_rows[k] * 8, 8), 8), :], dst_ref=y_in.at[k],
            send_sem=y_send.at[k], recv_sem=y_recv.at[k], device_id=y_peer[k], device_id_type=MESH)

    for k in range(3):
        y_copy(k).start()
    for k in range(3):
        y_copy(k).wait_recv()
    mine = pl.ds(pl.multiple_of(8 * sub, 8), 8)
    others = pl.ds(pl.multiple_of(8 * (1 - sub), 8), 8)
    patch_v[mine, :] = y_out[pl.ds(pl.multiple_of(yh * 8, 8), 8), :] + y_in[0]
    patch_v[others, :] = y_in[1] + y_in[2]

    n_copy0.wait_send()
    wait_a_send(psi0, 0)
    wait_a_send(psi1, 2)
    for k in range(4):
        n_copy1(k).wait_send()

    @pl.when(is_wall)
    def _():
        for k in range(4):
            s_copy(k).wait_send()

    for k in range(4):
        c_copy(k).wait_send()
    for k in (0, 1, 3):
        x_copy(k).wait_send()
    for d in range(1, NZ):
        z_copy(d).wait_send()
    for k in range(3):
        y_copy(k).wait_send()
    state_copy.wait()


def local(
    adjoint_start, objective_grad, flux_jacobian, stab_block, precond_block,
    wall_weight, wall_geometry, face_patch, patch_slot,
):
    any_, vmem, smem = (pl.BlockSpec(memory_space=m) for m in (pl.ANY, pltpu.VMEM, pltpu.SMEM))
    dma = pltpu.SemaphoreType.DMA
    state, patch = pl.pallas_call(
        kernel,
        out_shape=(jax.ShapeDtypeStruct((NV, 256, 128), F32), jax.ShapeDtypeStruct((16, 128), F32)),
        in_specs=[any_, any_, any_, any_, any_, smem, any_, vmem, vmem],
        out_specs=(any_, vmem),
        scratch_shapes=[
            pltpu.VMEM((NV, 272, 128), F32),
            pltpu.VMEM((NV, 272, 128), F32),
            pltpu.VMEM((NV, 256, 128), F32),
            pltpu.VMEM((NV, 256, 128), F32),
            pltpu.VMEM((75, 256, 128), BF16),
            pltpu.VMEM((25, 256, 128), BF16),
            pltpu.VMEM((25, 256, 128), BF16),
            pltpu.VMEM((8192, 128), BF16),
            pltpu.VMEM((32, 256, 128), F32),
            pltpu.VMEM((1024, 4096), BF16),
            pltpu.VMEM((32, 128), jnp.int32),
            pltpu.VMEM((1024, 256), BF16),
            pltpu.VMEM((1024, 128), F32),
            pltpu.VMEM((NV, 32, 1, 128), F32),
            pltpu.VMEM((NV, 32, 1, 128), F32),
            pltpu.VMEM((NV, 32, 1, 128), F32),
            pltpu.VMEM((NV, 32, 1, 128), F32),
            pltpu.VMEM((2, 32, 128), F32),
            pltpu.VMEM((2, 32, 128), F32),
            pltpu.VMEM((4, 128, 128), F32),
            pltpu.VMEM((4, 128, 128), F32),
            pltpu.VMEM((4, 128, 128), F32),
            pltpu.VMEM((128, 128), F32),
            pltpu.VMEM((NZ - 1, 16, 128), F32),
            pltpu.VMEM((16, 128), F32),
            pltpu.VMEM((3, 8, 128), F32),
            dma((8,)), dma,
            dma((4,)), dma((4,)),
            dma((5,)), dma((5,)),
            dma((4,)), dma((4,)),
            dma((4,)), dma((4,)),
            dma((4,)), dma((4,)),
            dma((NZ - 1,)), dma((NZ - 1,)),
            dma((3,)), dma((3,)),
        ],
        compiler_params=pltpu.CompilerParams(
            collective_id=0, has_side_effects=True, vmem_limit_bytes=60 * 1024 * 1024),
    )(
        adjoint_start.reshape(NV, 256, 128),
        objective_grad.reshape(NV, 256, 128),
        flux_jacobian.reshape(75, 256, 128),
        stab_block.reshape(25, 256, 128),
        precond_block.reshape(25, 256, 128),
        wall_weight,
        wall_geometry.reshape(8192, 128),
        face_patch.reshape(32, 128),
        patch_slot.reshape(16, 128),
    )
    return state.reshape(NV, 32, 8, 128), patch


def solution(mesh):
    return jax.shard_map(
        local,
        mesh=mesh,
        in_specs=(
            P(None, "blk", "sub", None),
            P(None, "blk", "sub", None),
            P(None, None, None, "blk", "sub", None),
            P(None, None, "blk", "sub", None),
            P(None, None, "blk", "sub", None),
            P(),
            P("blk", None, None),
            P("blk"),
            P(),
        ),
        out_specs=(P(None, "blk", "sub", None), P("blk", None)),
        check_vma=False,
    )
```

time: 787 us -> 50 us (0.06)
  waiting for transfers between devices: 667 us -> 0 us
  Pallas kernels: 0 us -> 44.5 us
  other arithmetic: 39.4 us -> 0 us
  local copies, waits for them, and re-layouts: 32.7 us -> 4.61 us
  starting transfers between devices: 21.3 us -> 0 us
  between operations: 14.5 us -> 0.64 us
    reduce_scatter x1 -> x0, waiting for transfers between devices: 659 us -> none  [local(): lax.psum_scatter(paired, 'blk', scatter_dimension=0, tiled=True)]
    pallas_call x0 -> x1, Pallas kernels: none -> 44.5 us  [local(): pl.pallas_call(kernel, out_shape=(jax.ShapeDtypeStruct((NV, 256, 128), F3...]
    scatter-add x1 -> x0, other arithmetic: 23.9 us -> none  [patch_partial(): jax.ops.segment_sum(contribution, slots, num_segments=patch_slot.shape[0])]
    gather x1 -> x0, local copies, waits for them, and re-layouts: 23 us -> none  [patch_partial(): slots = patch_slot[patch_rows]]
    ppermute x8 -> x0, starting transfers between devices: 21.2 us -> none  [the longest x4 14.6 us: padded_2(): before = lax.ppermute(last, axis, up)]
    reduce_sum x7 -> x0, other arithmetic: 10.3 us -> none  [the longest x4 9.32 us: transposed(): return jnp.sum(matrix * field[:, None], axis=0)]
  transfers between devices with their start and end apart: 9 -> 0, of which waited for: 4 -> 0; matrix products, arithmetic and copies ran while one was open for 4% -> 0% of each run, Pallas kernels for 0% -> 0%
where the time goes in v1:
time: 50 us; the launch traced here: 49.8 us
  Pallas kernels  44.5 us (89%)
  local copies, waits for them, and re-layouts  4.61 us (9%)
  between operations  0.64 us (1%)
    pallas_call x1, Pallas kernels, local(): pl.pallas_call(kernel, out_shape=(jax.ShapeDtypeStruct((NV, 256, 128), F3...  44.5 us
    unnamed x3, local copies, waits for them, and re-layouts  4.61 us

profile of v1, /device:TPU:1, one launch (start us, length us, event | category | flops | bytes accessed | tf_op | source)
XLA Modules:
  0.0 49.8 jit_solution(353679296210330973)
XLA Ops:
  0.6 1.4 %copy.11.weight_s = f32[5,2]{1,0:T(8,128)} copy(f32[5,2]{0,1:T(2,128)} %param.14) | data formatting | bytes 80 | tf_op args[5]
  2.0 44.5 %shard_map.104 = (f32[5,256,128]{2,1,0:T(8,128)}, f32[16,128]{1,0:T(8,128)}) custom-call(f32[5,256,128]{2,1,0:T(8,128)} %bitcast.13, f32[5,256,128]{2,1,0:T(8,128)} %bitcast.14, bf16[75,256,128]{2,1,0:T(8,128)(2,1)} %bitcast.9, bf16[25,256,128]{2,1,0:T(8,128)(2,1)} %bitcast.11, bf16[25,256,128]{2,1,0:T(8,128)(2,1)} %bitcast.12, f32[5,2]{1,0:T(8,128)} %copy.11.weight_s, ...), custom_call_target="tpu_custom_call" | custom-call | tf_op jit(solution)/shard_map/pallas_call | solution.py:432
  46.5 2.0 %copy.14 = f32[5,32,8,128]{3,2,1,0:T(8,128)} copy(f32[5,32,8,128]{3,2,1,0:T(8,128)} %bitcast.15) | data formatting | bytes 1310720
  48.5 1.3 %copy.15 = f32[16,128]{1,0:T(8,128)} copy(f32[16,128]{1,0:T(8,128)} %get-tuple-element.9) | data formatting | bytes 16384

commit v2 on v1

--- a/solution.py
+++ b/solution.py
@@ -12,16 +12,19 @@
 BF16 = jnp.bfloat16
 
 NV = 5
+PARTS = ((16, 80), (0, 16), (240, 256), (80, 176), (176, 240))
+PART_OF = ((0,), (1, 2), (3,), (4,))
+GHOSTS = ((4, 12), (0, 4), (12, 24), (24, 32))
 NX, NZ = 4, 8
 
 
 def kernel(
-    start_h, grad_h, jac_h, stab_h, prec_h, weight_s, geom_h, face_v, slot_v,
+    start_h, grad_h, jac_h, stab_h, prec_h, weight_h, geom_h, face_h, slot_h,
     state_h, patch_v,
-    psi0, psi1, psi2, grad, jac, stab, prec, geom, geom32, onehot, key, contrib, acc,
+    psi0, psi1, psi2, grad, jac, stab, prec, geom, weight_s, face_v, slot_v, geom32, onehot, key, contrib, acc,
     nsend0, nrecv0, nsend1, nrecv1, sens_loc, sens,
     core_in, x_out, x_in, z_out, z_in, y_out, y_in,
-    load_sem, out_sem, a_send, a_recv, n_send, n_recv, s_send, s_recv,
+    load_sem, part_sem, out_sem, a_send, a_recv, n0_send, n0_recv, n_send, n_recv, s_send, s_recv,
     c_send, c_recv, x_send, x_recv, z_send, z_recv, y_send, y_recv,
 ):
     blk, sub = lax.axis_index("blk"), lax.axis_index("sub")
@@ -43,19 +46,6 @@
     other = jnp.where(core == 1, blk + 1, blk - 1)
     has_other = jnp.logical_and(other >= 0, other < n_blk)
 
-    loads = [
-        pltpu.make_async_copy(start_h, psi0.at[:, 8:264, :], load_sem.at[0]),
-        pltpu.make_async_copy(geom_h, geom, load_sem.at[1]),
-        pltpu.make_async_copy(grad_h, grad, load_sem.at[2]),
-        pltpu.make_async_copy(jac_h.at[0:25], jac.at[0:25], load_sem.at[3]),
-        pltpu.make_async_copy(jac_h.at[25:50], jac.at[25:50], load_sem.at[4]),
-        pltpu.make_async_copy(jac_h.at[50:75], jac.at[50:75], load_sem.at[5]),
-        pltpu.make_async_copy(stab_h, stab, load_sem.at[6]),
-        pltpu.make_async_copy(prec_h, prec, load_sem.at[7]),
-    ]
-    for load in loads:
-        load.start()
-
     barrier = pltpu.get_barrier_semaphore()
     peers = [core_peer] + x_peer[1:] + z_peer[1:] + y_peer
     for peer in peers:
@@ -65,6 +55,27 @@
     def _():
         pl.semaphore_signal(barrier, inc=1, device_id=(other, sub), device_id_type=MESH)
 
+    loads = [
+        pltpu.make_async_copy(start_h, psi0.at[:, 8:264, :], load_sem.at[0]),
+        pltpu.make_async_copy(face_h, face_v, load_sem.at[1]),
+        pltpu.make_async_copy(slot_h, slot_v, load_sem.at[2]),
+        pltpu.make_async_copy(weight_h, weight_s, load_sem.at[3]),
+        pltpu.make_async_copy(geom_h, geom, load_sem.at[4]),
+    ]
+    parts = []
+    for n, (low, high) in enumerate(PARTS):
+        rows = slice(low, high)
+        parts.append([
+            pltpu.make_async_copy(far.at[:, rows, :], near.at[:, rows, :], part_sem.at[4 * n + j])
+            for j, (far, near) in enumerate(((jac_h, jac), (stab_h, stab), (prec_h, prec), (grad_h, grad)))
+        ])
+    for load in loads[:4]:
+        load.start()
+    for part in parts:
+        for load in part:
+            load.start(priority=1)
+    loads[4].start(priority=1)
+
     zero_plane = jnp.zeros((NV, 8, 128), F32)
     for buf in (psi0, psi1):
         @pl.when(jnp.logical_not(has_left))
@@ -80,9 +91,10 @@
     def edge_row(plane):
         return jnp.where(sub == 0, plane[7:8], plane[0:1])
 
-    def pick0(a, carry):
+    def pick0(q, carry):
+        a = lax.rem(q + 30, 32)
         for v in range(NV):
-            nsend0[v, a] = edge_row(psi0[v, pl.ds(pl.multiple_of(8 * a + 8, 8), 8), :])
+            nsend0[v, q] = edge_row(psi0[v, pl.ds(pl.multiple_of(8 * a + 8, 8), 8), :])
         return carry
 
     lax.fori_loop(0, 32, pick0, 0)
@@ -133,12 +145,18 @@
         def _():
             left.wait_send()
 
-    n_copy0 = pltpu.make_async_remote_copy(
-        src_ref=nsend0, dst_ref=nrecv0, send_sem=n_send.at[4], recv_sem=n_recv.at[4],
-        device_id=partner, device_id_type=MESH)
-    n_copy0.start()
+    n_copy0 = [
+        pltpu.make_async_remote_copy(
+            src_ref=nsend0.at[:, low:high], dst_ref=nrecv0.at[:, low:high],
+            send_sem=n0_send.at[n], recv_sem=n0_recv.at[n], device_id=partner, device_id_type=MESH)
+        for n, (low, high) in enumerate(GHOSTS)]
+    n_copy0[0].start()
     start_a(psi0, 0)
-
+    for copy in n_copy0[1:]:
+        copy.start()
+
+    loads[1].wait()
+    loads[2].wait()
     table = slot_v[...]
     for g in range(4):
         patch = face_v[8 * g:8 * g + 8, :]
@@ -152,24 +170,19 @@
         row = (core_ << 9) + (x_ << 7) + (z_ << 4) + (yh_ << 3) + j_
         key[8 * g:8 * g + 8, :] = jnp.where(sub_ == sub, row, -1)
 
-    def fill(i, carry):
-        a = lax.rem(i + 6, 32)
-        k = jnp.broadcast_to(key[pl.ds(a, 1), :], (16, 128))
-        base = lax.broadcasted_iota(jnp.int32, (16, 128), 0)
+    def fill(q, carry):
+        k = jnp.broadcast_to(key[pl.ds(lax.rem(q + 2, 32), 1), :], (16, 128))
+        same = (k & 15) == lax.broadcasted_iota(jnp.int32, (16, 128), 0)
+        tile = jnp.where(jnp.logical_and(same, k >= 0), k >> 4, -1).astype(F32).astype(BF16)
+        one, zero = jnp.ones((16, 128), BF16), jnp.zeros((16, 128), BF16)
         for m in range(64):
-            hit = (base + 16 * m) == k
-            onehot[16 * m:16 * m + 16, pl.ds(pl.multiple_of(i * 128, 128), 128)] = jnp.where(hit, 1.0, 0.0).astype(BF16)
-        return carry
-
-    lax.fori_loop(0, 32, fill, 0)
-
-    loads[1].wait()
+            onehot[16 * m:16 * m + 16, pl.ds(pl.multiple_of(q * 128, 128), 128)] = jnp.where(
+                tile == jnp.array(m, BF16), one, zero)
+        return carry
 
     def widen(a, carry):
         geom32[a] = geom[pl.ds(pl.multiple_of(a * 256, 256), 256), :].astype(F32)
         return carry
-
-    lax.fori_loop(0, 32, widen, 0)
 
     sub_iota = lax.broadcasted_iota(jnp.int32, (16, 128), 0) & 7
     lane_iota = lax.broadcasted_iota(jnp.int32, (16, 128), 1)
@@ -210,37 +223,46 @@
             result.append(psi[u] + step)
         return result
 
-    for load in loads[2:]:
-        load.wait()
-    n_copy0.wait_recv()
-    wait_a_recv(psi0, 0)
-
-    def n_copy1(k):
-        part = pl.ds(pl.multiple_of(8 * k, 8), 8)
+    def n_copy1(d):
+        part = pl.ds(4 * d, 4)
         return pltpu.make_async_remote_copy(
-            src_ref=nsend1.at[:, part], dst_ref=nrecv1.at[:, part], send_sem=n_send.at[k], recv_sem=n_recv.at[k],
+            src_ref=nsend1.at[:, part], dst_ref=nrecv1.at[:, part], send_sem=n_send.at[d], recv_sem=n_recv.at[d],
             device_id=partner, device_id_type=MESH)
 
-    def first_part(k, carry):
-        def pair(i, carry):
-            p = lax.rem(i + 15, 16)
-            new = sweep_pair(p, psi0, nrecv0, 2 * p)
+    def first_part(s, carry):
+        d = jnp.where(s < 2, s + 1, jnp.where(s == 2, 0, s))
+
+        for n, step in enumerate((0, 2, 3, 6)):
+            @pl.when(s == step)
+            def _():
+                for part in PART_OF[n]:
+                    for load in parts[part]:
+                        load.wait()
+                n_copy0[n].wait_recv()
+                if n == 1:
+                    wait_a_recv(psi0, 0)
+
+        def pair(j, carry):
+            p = lax.rem(2 * d + j + 15, 16)
+            row = 4 * d + 2 * j
+            new = sweep_pair(p, psi0, nrecv0, row)
             for v in range(NV):
                 psi1[v, pl.ds(pl.multiple_of(16 * p + 8, 8), 16), :] = new[v]
-                nsend1[v, 2 * i] = edge_row(new[v][0:8])
-                nsend1[v, 2 * i + 1] = edge_row(new[v][8:16])
+                nsend1[v, row] = edge_row(new[v][0:8])
+                nsend1[v, row + 1] = edge_row(new[v][8:16])
             return carry
 
-        lax.fori_loop(4 * k, 4 * k + 4, pair, 0)
-        n_copy1(k).start()
-
-        @pl.when(k == 0)
+        lax.fori_loop(0, 2, pair, 0)
+        n_copy1(d).start()
+
+        @pl.when(s == 2)
         def _():
             start_a(psi1, 2)
 
         return carry
 
-    lax.fori_loop(0, 4, first_part, 0)
+    lax.fori_loop(0, 8, first_part, 0)
+    lax.fori_loop(0, 32, fill, 0)
 
     is_wall = core == sub
     not_wall = jnp.logical_not(is_wall)
@@ -254,39 +276,46 @@
     def wall_row(plane):
         return jnp.where(sub == 0, plane[0:1], plane[7:8])
 
-    def second_part(k, carry):
-        n_copy1(lax.rem(k + 1, 4)).wait_recv()
-
-        @pl.when(k == 3)
+    loads[3].wait()
+
+    def second_part(s, carry):
+        d = lax.rem(s + 1, 8)
+        n_copy1(d).wait_recv()
+
+        @pl.when(s == 7)
         def _():
             wait_a_recv(psi1, 2)
 
-        def pair(i, carry):
-            p = lax.rem(i + 3, 16)
-            new = sweep_pair(p, psi1, nrecv1, 2 * lax.rem(i + 4, 16))
+        def pair(j, carry):
+            p = lax.rem(2 * d + j + 15, 16)
+            q = 4 * s + 2 * j
+            new = sweep_pair(p, psi1, nrecv1, 4 * d + 2 * j)
             for v in range(NV):
                 psi2[v, pl.ds(pl.multiple_of(16 * p, 16), 16), :] = new[v]
             for j in range(2):
-                total = weight_s[0, j] * new[0]
+                total = weight_s[j, 0] * new[0]
                 for v in range(1, NV):
-                    total = total + weight_s[v, j] * new[v]
-                sens_loc[j, pl.ds(2 * i, 1), :] = wall_row(total[0:8])
-                sens_loc[j, pl.ds(2 * i + 1, 1), :] = wall_row(total[8:16])
+                    total = total + weight_s[j, v] * new[v]
+                sens_loc[j, pl.ds(q, 1), :] = wall_row(total[0:8])
+                sens_loc[j, pl.ds(q + 1, 1), :] = wall_row(total[8:16])
             return carry
 
-        lax.fori_loop(4 * k, 4 * k + 4, pair, 0)
-
-        @pl.when(is_wall)
-        def _():
+        lax.fori_loop(0, 2, pair, 0)
+
+        @pl.when(jnp.logical_and(is_wall, lax.rem(s, 2) == 1))
+        def _():
+            k = s // 2
             s_copy(k).start()
             part = pl.ds(pl.multiple_of(8 * k, 8), 8)
             sens[:, part, :] = sens_loc[:, part, :]
 
         return carry
 
-    lax.fori_loop(0, 4, second_part, 0)
+    lax.fori_loop(0, 8, second_part, 0)
     state_copy = pltpu.make_async_copy(psi2, state_h, out_sem)
     state_copy.start()
+    loads[4].wait()
+    lax.fori_loop(0, 32, widen, 0)
 
     def make_contrib(k):
         @pl.when(not_wall)
@@ -297,7 +326,7 @@
         pressure = jnp.transpose(sens[0, part, :])
         shear = jnp.transpose(sens[1, part, :])
         for r in range(8):
-            a = lax.rem(8 * k + 6 + r, 32)
+            a = lax.rem(8 * k + 2 + r, 32)
             g0 = geom32[a, pl.ds(0, 128, 2), :]
             g1 = geom32[a, pl.ds(1, 128, 2), :]
             c = pressure[:, r:r + 1] * g0 + shear[:, r:r + 1] * g1
@@ -307,7 +336,7 @@
             contrib[128 * r:128 * r + 128, 128:256] = lo
 
     def product(row, k):
-        part = onehot[pl.ds(pl.multiple_of(row, 128), 128), pl.ds(pl.multiple_of(k * 1024, 1024), 1024)]
+        part = onehot[pl.ds(pl.multiple_of(row, 512), 512), pl.ds(pl.multiple_of(k * 1024, 1024), 1024)]
         both = jnp.dot(part, contrib[...], preferred_element_type=F32)
         return both[:, 0:128] + both[:, 128:256]
 
@@ -317,18 +346,18 @@
         make_contrib(k)
 
         def block(m, carry):
-            rows = pl.ds(pl.multiple_of(m * 128, 128), 128)
-            acc[rows, :] += product(m * 128, k)
+            rows = pl.ds(pl.multiple_of(m * 512, 512), 512)
+            acc[rows, :] += product(m * 512, k)
             return carry
 
-        lax.fori_loop(0, 8, block, 0)
+        lax.fori_loop(0, 2, block, 0)
         return carry
 
     lax.fori_loop(0, 3, quarter, 0)
     make_contrib(3)
 
     def order(k):
-        return lax.rem(k + 2, 4)
+        return jnp.where(k == 0, 2, jnp.where(k == 1, 3, 3 - k)) if not isinstance(k, int) else (2, 3, 1, 0)[k]
 
     def c_copy(k):
         start = (1 - core) * 512 + lax.rem(x + order(k), NX) * 128
@@ -342,21 +371,17 @@
             src_ref=x_out.at[k], dst_ref=x_in.at[k],
             send_sem=x_send.at[k], recv_sem=x_recv.at[k], device_id=peer, device_id_type=MESH)
 
-    def away(k, carry):
-        start = (1 - core) * 512 + lax.rem(x + order(k), NX) * 128
-        rows = pl.ds(pl.multiple_of(start, 128), 128)
-        acc[rows, :] += product(start, 3)
+    rows = pl.ds(pl.multiple_of((1 - core) * 512, 512), 512)
+    acc[rows, :] += product((1 - core) * 512, 3)
+    for k in range(4):
         c_copy(k).start()
-        return carry
-
-    lax.fori_loop(0, 4, away, 0)
+    rows = pl.ds(pl.multiple_of(core * 512, 512), 512)
+    acc[rows, :] += product(core * 512, 3)
 
     def kept(k, carry):
         start = core * 512 + lax.rem(x + order(k), NX) * 128
-        rows = pl.ds(pl.multiple_of(start, 128), 128)
-        mine = acc[rows, :] + product(start, 3)
         c_copy(k).wait_recv()
-        x_out[k] = mine + core_in[k]
+        x_out[k] = acc[pl.ds(pl.multiple_of(start, 128), 128), :] + core_in[k]
 
         @pl.when(order(k) != 0)
         def _():
@@ -365,9 +390,9 @@
         return carry
 
     lax.fori_loop(0, 4, kept, 0)
-    for k in (1, 3, 0):
+    for k in (1, 2, 0):
         x_copy(k).wait_recv()
-    z_out[...] = x_out[2] + x_in[0] + x_in[1] + x_in[3]
+    z_out[...] = x_out[3] + x_in[0] + x_in[1] + x_in[2]
 
     def z_copy(d):
         dest = lax.rem(z + d, NZ)
@@ -401,11 +426,12 @@
     patch_v[mine, :] = y_out[pl.ds(pl.multiple_of(yh * 8, 8), 8), :] + y_in[0]
     patch_v[others, :] = y_in[1] + y_in[2]
 
-    n_copy0.wait_send()
+    for copy in n_copy0:
+        copy.wait_send()
     wait_a_send(psi0, 0)
     wait_a_send(psi1, 2)
-    for k in range(4):
-        n_copy1(k).wait_send()
+    for d in range(8):
+        n_copy1(d).wait_send()
 
     @pl.when(is_wall)
     def _():
@@ -414,7 +440,7 @@
 
     for k in range(4):
         c_copy(k).wait_send()
-    for k in (0, 1, 3):
+    for k in range(3):
         x_copy(k).wait_send()
     for d in range(1, NZ):
         z_copy(d).wait_send()
@@ -423,16 +449,29 @@
     state_copy.wait()
 
 
+def hand_on(state_in, patch_in, state_out, patch_out, state, patch, in_sem, out_sem):
+    pieces = [(patch_in, patch, patch_out)] + [(state_in.at[v], state.at[v], state_out.at[v]) for v in range(NV)]
+    enter = [pltpu.make_async_copy(a, b, in_sem.at[n]) for n, (a, b, _) in enumerate(pieces)]
+    leave = [pltpu.make_async_copy(b, c, out_sem.at[n]) for n, (_, b, c) in enumerate(pieces)]
+    for copy in enter:
+        copy.start()
+    for n, copy in enumerate(enter):
+        copy.wait()
+        leave[n].start()
+    for copy in leave:
+        copy.wait()
+
+
 def local(
     adjoint_start, objective_grad, flux_jacobian, stab_block, precond_block,
     wall_weight, wall_geometry, face_patch, patch_slot,
 ):
-    any_, vmem, smem = (pl.BlockSpec(memory_space=m) for m in (pl.ANY, pltpu.VMEM, pltpu.SMEM))
+    any_, vmem = (pl.BlockSpec(memory_space=m) for m in (pl.ANY, pltpu.VMEM))
     dma = pltpu.SemaphoreType.DMA
     state, patch = pl.pallas_call(
         kernel,
         out_shape=(jax.ShapeDtypeStruct((NV, 256, 128), F32), jax.ShapeDtypeStruct((16, 128), F32)),
-        in_specs=[any_, any_, any_, any_, any_, smem, any_, vmem, vmem],
+        in_specs=[any_] * 9,
         out_specs=(any_, vmem),
         scratch_shapes=[
             pltpu.VMEM((NV, 272, 128), F32),
@@ -443,6 +482,9 @@
             pltpu.VMEM((25, 256, 128), BF16),
             pltpu.VMEM((25, 256, 128), BF16),
             pltpu.VMEM((8192, 128), BF16),
+            pltpu.SMEM((2, NV), F32),
+            pltpu.VMEM((32, 128), jnp.int32),
+            pltpu.VMEM((16, 128), jnp.int32),
             pltpu.VMEM((32, 256, 128), F32),
             pltpu.VMEM((1024, 4096), BF16),
             pltpu.VMEM((32, 128), jnp.int32),
@@ -461,9 +503,9 @@
             pltpu.VMEM((NZ - 1, 16, 128), F32),
             pltpu.VMEM((16, 128), F32),
             pltpu.VMEM((3, 8, 128), F32),
-            dma((8,)), dma,
+            dma((5,)), dma((4 * len(PARTS),)), dma,
             dma((4,)), dma((4,)),
-            dma((5,)), dma((5,)),
+            dma((4,)), dma((4,)), dma((8,)), dma((8,)),
             dma((4,)), dma((4,)),
             dma((4,)), dma((4,)),
             dma((4,)), dma((4,)),
@@ -478,11 +520,19 @@
         flux_jacobian.reshape(75, 256, 128),
         stab_block.reshape(25, 256, 128),
         precond_block.reshape(25, 256, 128),
-        wall_weight,
+        wall_weight.T,
         wall_geometry.reshape(8192, 128),
         face_patch.reshape(32, 128),
         patch_slot.reshape(16, 128),
     )
+    state, patch = pl.pallas_call(
+        hand_on,
+        out_shape=(jax.ShapeDtypeStruct(state.shape, F32), jax.ShapeDtypeStruct(patch.shape, F32)),
+        in_specs=[any_, any_],
+        out_specs=(any_, any_),
+        scratch_shapes=[pltpu.VMEM((NV, 256, 128), F32), pltpu.VMEM((16, 128), F32), dma((6,)), dma((6,))],
+        compiler_params=pltpu.CompilerParams(vmem_limit_bytes=60 * 1024 * 1024),
+    )(state, patch)
     return state.reshape(NV, 32, 8, 128), patch
 
 

time: 50 us -> 45.6 us (0.912)
  local copies, waits for them, and re-layouts: 4.61 us -> 0 us
    unnamed x3 -> x0, local copies, waits for them, and re-layouts: 4.61 us -> none
    pallas_call x0 -> x1, Pallas kernels: none -> 1.94 us  [local(): pl.pallas_call(hand_on, out_shape=(jax.ShapeDtypeStruct(state.shape, F32)...]
    pallas_call x1, Pallas kernels: 44.5 us -> 42.8 us  [local(): pl.pallas_call(kernel, out_shape=(jax.ShapeDtypeStruct((NV, 256, 128), F3...]
where the time goes in v2:
time: 45.6 us; the launch traced here: 45.4 us
  Pallas kernels  44.8 us (98%)
  between operations  0.64 us (1%)
    pallas_call x1, Pallas kernels, local(): pl.pallas_call(kernel, out_shape=(jax.ShapeDtypeStruct((NV, 256, 128), F3...  42.8 us
    pallas_call x1, Pallas kernels, local(): pl.pallas_call(hand_on, out_shape=(jax.ShapeDtypeStruct(state.shape, F32)...  1.94 us

profile of v2, /device:TPU:1, one launch (start us, length us, event | category | flops | bytes accessed | tf_op | source)
XLA Modules:
  0.0 45.4 jit_solution(1651896014810866565)
XLA Ops:
  0.6 42.8 %shard_map.104 = (f32[5,256,128]{2,1,0:T(8,128)}, f32[16,128]{1,0:T(8,128)}) custom-call(f32[5,256,128]{2,1,0:T(8,128)} %bitcast.14, f32[5,256,128]{2,1,0:T(8,128)} %bitcast.15, bf16[75,256,128]{2,1,0:T(8,128)(2,1)} %bitcast.10, bf16[25,256,128]{2,1,0:T(8,128)(2,1)} %bitcast.12, bf16[25,256,128]{2,1,0:T(8,128)(2,1)} %bitcast.13, f32[2,5]{1,0:T(2,128)} %bitcast.18, ...), custom_call_target="tpu_custom_call" | custom-call | tf_op jit(solution)/shard_map/pallas_call | solution.py:471
  43.5 1.9 %shard_map.105 = (f32[5,256,128]{2,1,0:T(8,128)}, f32[16,128]{1,0:T(8,128)}) custom-call(f32[5,256,128]{2,1,0:T(8,128)} %get-tuple-element.6.state_in, f32[16,128]{1,0:T(8,128)} %get-tuple-element.7.patch_in), custom_call_target="tpu_custom_call" | custom-call | tf_op jit(solution)/shard_map/pallas_call | solution.py:528

commit v3 on v2

--- a/solution.py
+++ b/solution.py
@@ -23,9 +23,9 @@
     state_h, patch_v,
     psi0, psi1, psi2, grad, jac, stab, prec, geom, weight_s, face_v, slot_v, geom32, onehot, key, contrib, acc,
     nsend0, nrecv0, nsend1, nrecv1, sens_loc, sens,
-    core_in, x_out, x_in, z_out, z_in, y_out, y_in,
+    core_in, ax_out, ax_in, az_out, az_in, bz_out, bz_in, bx_out, bx_in, y_out, y_in,
     load_sem, part_sem, out_sem, a_send, a_recv, n0_send, n0_recv, n_send, n_recv, s_send, s_recv,
-    c_send, c_recv, x_send, x_recv, z_send, z_recv, y_send, y_recv,
+    c_send, c_recv, ax_send, ax_recv, az_send, az_recv, bz_send, bz_recv, bx_send, bx_recv, y_send, y_recv,
 ):
     blk, sub = lax.axis_index("blk"), lax.axis_index("sub")
     n_blk = lax.axis_size("blk")
@@ -167,7 +167,8 @@
             found = jnp.where(high == j, jnp.take_along_axis(line, lane, axis=1), found)
         j_, sub_, core_ = found & 7, (found >> 3) & 1, (found >> 4) & 1
         z_, x_, yh_ = (found >> 5) & 7, (found >> 8) & 3, (found >> 10) & 1
-        row = (core_ << 9) + (x_ << 7) + (z_ << 4) + (yh_ << 3) + j_
+        place = jnp.where(yh_ == 0, (x_ << 6) + (z_ << 3), (z_ << 5) + (x_ << 3))
+        row = (core_ << 9) + (yh_ << 8) + place + j_
         key[8 * g:8 * g + 8, :] = jnp.where(sub_ == sub, row, -1)
 
     def fill(q, carry):
@@ -335,8 +336,8 @@
             contrib[128 * r:128 * r + 128, 0:128] = hi
             contrib[128 * r:128 * r + 128, 128:256] = lo
 
-    def product(row, k):
-        part = onehot[pl.ds(pl.multiple_of(row, 512), 512), pl.ds(pl.multiple_of(k * 1024, 1024), 1024)]
+    def product(row, rows, k):
+        part = onehot[pl.ds(pl.multiple_of(row, 512), rows), pl.ds(pl.multiple_of(k * 1024, 1024), 1024)]
         both = jnp.dot(part, contrib[...], preferred_element_type=F32)
         return both[:, 0:128] + both[:, 128:256]
 
@@ -344,71 +345,62 @@
 
     def quarter(k, carry):
         make_contrib(k)
-
-        def block(m, carry):
-            rows = pl.ds(pl.multiple_of(m * 512, 512), 512)
-            acc[rows, :] += product(m * 512, k)
-            return carry
-
-        lax.fori_loop(0, 2, block, 0)
+        acc[...] += product(0, 1024, k)
         return carry
 
     lax.fori_loop(0, 3, quarter, 0)
     make_contrib(3)
 
-    def order(k):
-        return jnp.where(k == 0, 2, jnp.where(k == 1, 3, 3 - k)) if not isinstance(k, int) else (2, 3, 1, 0)[k]
-
-    def c_copy(k):
-        start = (1 - core) * 512 + lax.rem(x + order(k), NX) * 128
+    def c_copy(h):
         return pltpu.make_async_remote_copy(
-            src_ref=acc.at[pl.ds(pl.multiple_of(start, 128), 128), :], dst_ref=core_in.at[k],
-            send_sem=c_send.at[k], recv_sem=c_recv.at[k], device_id=core_peer, device_id_type=MESH)
-
-    def x_copy(k):
-        peer = (at(yh, lax.rem(x + order(k), NX), z, core), sub)
-        return pltpu.make_async_remote_copy(
-            src_ref=x_out.at[k], dst_ref=x_in.at[k],
-            send_sem=x_send.at[k], recv_sem=x_recv.at[k], device_id=peer, device_id_type=MESH)
-
-    rows = pl.ds(pl.multiple_of((1 - core) * 512, 512), 512)
-    acc[rows, :] += product((1 - core) * 512, 3)
-    for k in range(4):
-        c_copy(k).start()
-    rows = pl.ds(pl.multiple_of(core * 512, 512), 512)
-    acc[rows, :] += product(core * 512, 3)
-
-    def kept(k, carry):
-        start = core * 512 + lax.rem(x + order(k), NX) * 128
-        c_copy(k).wait_recv()
-        x_out[k] = acc[pl.ds(pl.multiple_of(start, 128), 128), :] + core_in[k]
-
-        @pl.when(order(k) != 0)
-        def _():
-            x_copy(k).start()
-
-        return carry
-
-    lax.fori_loop(0, 4, kept, 0)
-    for k in (1, 2, 0):
-        x_copy(k).wait_recv()
-    z_out[...] = x_out[3] + x_in[0] + x_in[1] + x_in[2]
-
-    def z_copy(d):
-        dest = lax.rem(z + d, NZ)
-        peer = (at(yh, x, dest, core), sub)
-        return pltpu.make_async_remote_copy(
-            src_ref=z_out.at[pl.ds(pl.multiple_of(dest * 16, 16), 16), :], dst_ref=z_in.at[d - 1],
-            send_sem=z_send.at[d - 1], recv_sem=z_recv.at[d - 1], device_id=peer, device_id_type=MESH)
-
-    for d in (4, 3, 5, 2, 6, 1, 7):
-        z_copy(d).start()
-    for d in range(1, NZ):
-        z_copy(d).wait_recv()
-    total = z_out[pl.ds(pl.multiple_of(z * 16, 16), 16), :]
-    for d in range(NZ - 1):
-        total = total + z_in[d]
-    y_out[...] = total
+            src_ref=acc.at[pl.ds(pl.multiple_of((1 - core) * 512 + h * 256, 256), 256), :], dst_ref=core_in.at[h],
+            send_sem=c_send.at[h], recv_sem=c_recv.at[h], device_id=core_peer, device_id_type=MESH)
+
+    def spread(out, into, send, recv, peer, place, size):
+        def copy(d):
+            dest = lax.rem(place + d, size)
+            rows = out.shape[0] // size
+            return pltpu.make_async_remote_copy(
+                src_ref=out.at[pl.ds(pl.multiple_of(dest * rows, rows), rows), :], dst_ref=into.at[d - 1],
+                send_sem=send.at[d - 1], recv_sem=recv.at[d - 1], device_id=peer[d], device_id_type=MESH)
+        return copy
+
+    ax_copy = spread(ax_out, ax_in, ax_send, ax_recv, x_peer, x, NX)
+    az_copy = spread(az_out, az_in, az_send, az_recv, z_peer, z, NZ)
+    bz_copy = spread(bz_out, bz_in, bz_send, bz_recv, z_peer, z, NZ)
+    bx_copy = spread(bx_out, bx_in, bx_send, bx_recv, x_peer, x, NX)
+    x_order, z_order = (2, 3, 1), (4, 3, 5, 2, 6, 1, 7)
+
+    def gathered(out, into, copy, place, size):
+        rows = out.shape[0] // size
+        for d in range(1, size):
+            copy(d).wait_recv()
+        total = out[pl.ds(pl.multiple_of(place * rows, rows), rows), :]
+        for d in range(1, size):
+            total = total + into[d - 1]
+        return total
+
+    acc[pl.ds(pl.multiple_of((1 - core) * 512, 512), 512), :] += product((1 - core) * 512, 512, 3)
+    for h in (1, 0):
+        c_copy(h).start()
+    acc[pl.ds(pl.multiple_of(core * 512, 512), 512), :] += product(core * 512, 512, 3)
+
+    c_copy(1).wait_recv()
+    bz_out[...] = acc[pl.ds(pl.multiple_of(core * 512 + 256, 256), 256), :] + core_in[1]
+    for d in z_order:
+        bz_copy(d).start()
+    c_copy(0).wait_recv()
+    ax_out[...] = acc[pl.ds(pl.multiple_of(core * 512, 256), 256), :] + core_in[0]
+    for d in x_order:
+        ax_copy(d).start()
+    az_out[...] = gathered(ax_out, ax_in, ax_copy, x, NX)
+    for d in z_order:
+        az_copy(d).start()
+    bx_out[...] = gathered(bz_out, bz_in, bz_copy, z, NZ)
+    for d in x_order:
+        bx_copy(d).start()
+    y_out[8:16, :] = gathered(bx_out, bx_in, bx_copy, x, NX)
+    y_out[0:8, :] = gathered(az_out, az_in, az_copy, z, NZ)
 
     y_rows = [1 - yh, 1 - yh, yh]
 
@@ -438,12 +430,14 @@
         for k in range(4):
             s_copy(k).wait_send()
 
-    for k in range(4):
-        c_copy(k).wait_send()
-    for k in range(3):
-        x_copy(k).wait_send()
+    for h in range(2):
+        c_copy(h).wait_send()
+    for d in range(1, NX):
+        ax_copy(d).wait_send()
+        bx_copy(d).wait_send()
     for d in range(1, NZ):
-        z_copy(d).wait_send()
+        az_copy(d).wait_send()
+        bz_copy(d).wait_send()
     for k in range(3):
         y_copy(k).wait_send()
     state_copy.wait()
@@ -496,20 +490,24 @@
             pltpu.VMEM((NV, 32, 1, 128), F32),
             pltpu.VMEM((2, 32, 128), F32),
             pltpu.VMEM((2, 32, 128), F32),
-            pltpu.VMEM((4, 128, 128), F32),
-            pltpu.VMEM((4, 128, 128), F32),
-            pltpu.VMEM((4, 128, 128), F32),
-            pltpu.VMEM((128, 128), F32),
-            pltpu.VMEM((NZ - 1, 16, 128), F32),
+            pltpu.VMEM((2, 256, 128), F32),
+            pltpu.VMEM((256, 128), F32),
+            pltpu.VMEM((NX - 1, 64, 128), F32),
+            pltpu.VMEM((64, 128), F32),
+            pltpu.VMEM((NZ - 1, 8, 128), F32),
+            pltpu.VMEM((256, 128), F32),
+            pltpu.VMEM((NZ - 1, 32, 128), F32),
+            pltpu.VMEM((32, 128), F32),
+            pltpu.VMEM((NX - 1, 8, 128), F32),
             pltpu.VMEM((16, 128), F32),
             pltpu.VMEM((3, 8, 128), F32),
             dma((5,)), dma((4 * len(PARTS),)), dma,
             dma((4,)), dma((4,)),
             dma((4,)), dma((4,)), dma((8,)), dma((8,)),
             dma((4,)), dma((4,)),
-            dma((4,)), dma((4,)),
-            dma((4,)), dma((4,)),
-            dma((NZ - 1,)), dma((NZ - 1,)),
+            dma((2,)), dma((2,)),
+            dma((NX - 1,)), dma((NX - 1,)), dma((NZ - 1,)), dma((NZ - 1,)),
+            dma((NZ - 1,)), dma((NZ - 1,)), dma((NX - 1,)), dma((NX - 1,)),
             dma((3,)), dma((3,)),
         ],
         compiler_params=pltpu.CompilerParams(

time: 45.6 us -> 43.7 us (0.958)
  Pallas kernels: 44.8 us -> 42.9 us
    pallas_call x1, Pallas kernels: 42.8 us -> 41 us  [local(): pl.pallas_call(kernel, out_shape=(jax.ShapeDtypeStruct((NV, 256, 128), F3...]
where the time goes in v3:
time: 43.7 us; the launch traced here: 43.6 us
  Pallas kernels  42.9 us (98%)
  between operations  0.64 us (1%)
    pallas_call x1, Pallas kernels, local(): pl.pallas_call(kernel, out_shape=(jax.ShapeDtypeStruct((NV, 256, 128), F3...  41 us
    pallas_call x1, Pallas kernels, local(): pl.pallas_call(hand_on, out_shape=(jax.ShapeDtypeStruct(state.shape, F32)...  1.94 us

profile of v3, /device:TPU:1, one launch (start us, length us, event | category | flops | bytes accessed | tf_op | source)
XLA Modules:
  0.0 43.6 jit_solution(16843635020001634831)
XLA Ops:
  0.6 41.0 %shard_map.104 = (f32[5,256,128]{2,1,0:T(8,128)}, f32[16,128]{1,0:T(8,128)}) custom-call(f32[5,256,128]{2,1,0:T(8,128)} %bitcast.14, f32[5,256,128]{2,1,0:T(8,128)} %bitcast.15, bf16[75,256,128]{2,1,0:T(8,128)(2,1)} %bitcast.10, bf16[25,256,128]{2,1,0:T(8,128)(2,1)} %bitcast.12, bf16[25,256,128]{2,1,0:T(8,128)(2,1)} %bitcast.13, f32[2,5]{1,0:T(2,128)} %bitcast.18, ...), custom_call_target="tpu_custom_call" | custom-call | tf_op jit(solution)/shard_map/pallas_call | solution.py:465
  41.6 1.9 %shard_map.105 = (f32[5,256,128]{2,1,0:T(8,128)}, f32[16,128]{1,0:T(8,128)}) custom-call(f32[5,256,128]{2,1,0:T(8,128)} %get-tuple-element.6.state_in, f32[16,128]{1,0:T(8,128)} %get-tuple-element.7.patch_in), custom_call_target="tpu_custom_call" | custom-call | tf_op jit(solution)/shard_map/pallas_call | solution.py:526

commit v4 on v3

--- a/solution.py
+++ b/solution.py
@@ -24,7 +24,7 @@
     psi0, psi1, psi2, grad, jac, stab, prec, geom, weight_s, face_v, slot_v, geom32, onehot, key, contrib, acc,
     nsend0, nrecv0, nsend1, nrecv1, sens_loc, sens,
     core_in, ax_out, ax_in, az_out, az_in, bz_out, bz_in, bx_out, bx_in, y_out, y_in,
-    load_sem, part_sem, out_sem, a_send, a_recv, n0_send, n0_recv, n_send, n_recv, s_send, s_recv,
+    rounds, load_sem, part_sem, out_sem, a_send, a_recv, n0_send, n0_recv, n_send, n_recv, s_send, s_recv,
     c_send, c_recv, ax_send, ax_recv, az_send, az_recv, bz_send, bz_recv, bx_send, bx_recv, y_send, y_recv,
 ):
     blk, sub = lax.axis_index("blk"), lax.axis_index("sub")
@@ -47,7 +47,8 @@
     has_other = jnp.logical_and(other >= 0, other < n_blk)
 
     barrier = pltpu.get_barrier_semaphore()
-    peers = [core_peer] + x_peer[1:] + z_peer[1:] + y_peer
+    near_z, near_x = [z_peer[1], z_peer[NZ - 1]], [x_peer[1], x_peer[NX - 1]]
+    peers = [core_peer, y_peer[1], partner] + near_x + near_z
     for peer in peers:
         pl.semaphore_signal(barrier, inc=1, device_id=peer, device_id_type=MESH)
 
@@ -154,6 +155,17 @@
     start_a(psi0, 0)
     for copy in n_copy0[1:]:
         copy.start()
+
+    around = [near_z + near_x + [partner], near_z, near_z]
+
+    def round_start(n):
+        for peer in around[n]:
+            pl.semaphore_signal(rounds.at[n], inc=1, device_id=peer, device_id_type=MESH)
+
+    def round_wait(n):
+        pl.semaphore_wait(rounds.at[n], len(around[n]))
+
+    round_start(0)
 
     loads[1].wait()
     loads[2].wait()
@@ -263,6 +275,8 @@
         return carry
 
     lax.fori_loop(0, 8, first_part, 0)
+    round_wait(0)
+    round_start(1)
     lax.fori_loop(0, 32, fill, 0)
 
     is_wall = core == sub
@@ -313,6 +327,8 @@
         return carry
 
     lax.fori_loop(0, 8, second_part, 0)
+    round_wait(1)
+    round_start(2)
     state_copy = pltpu.make_async_copy(psi2, state_h, out_sem)
     state_copy.start()
     loads[4].wait()
@@ -385,6 +401,7 @@
         c_copy(h).start()
     acc[pl.ds(pl.multiple_of(core * 512, 512), 512), :] += product(core * 512, 512, 3)
 
+    round_wait(2)
     c_copy(1).wait_recv()
     bz_out[...] = acc[pl.ds(pl.multiple_of(core * 512 + 256, 256), 256), :] + core_in[1]
     for d in z_order:
@@ -501,6 +518,7 @@
             pltpu.VMEM((NX - 1, 8, 128), F32),
             pltpu.VMEM((16, 128), F32),
             pltpu.VMEM((3, 8, 128), F32),
+            pltpu.SemaphoreType.REGULAR((3,)),
             dma((5,)), dma((4 * len(PARTS),)), dma,
             dma((4,)), dma((4,)),
             dma((4,)), dma((4,)), dma((8,)), dma((8,)),

time: 43.7 us -> 43 us (0.984)
  Pallas kernels: 42.9 us -> 42.3 us
    pallas_call x1, Pallas kernels: 41 us -> 40.3 us  [local(): pl.pallas_call(kernel, out_shape=(jax.ShapeDtypeStruct((NV, 256, 128), F3...]
where the time goes in v4:
time: 43 us; the launch traced here: 42.9 us
  Pallas kernels  42.3 us (98%)
  between operations  0.64 us (1%)
    pallas_call x1, Pallas kernels, local(): pl.pallas_call(kernel, out_shape=(jax.ShapeDtypeStruct((NV, 256, 128), F3...  40.3 us
    pallas_call x1, Pallas kernels, local(): pl.pallas_call(hand_on, out_shape=(jax.ShapeDtypeStruct(state.shape, F32)...  1.94 us

profile of v4, /device:TPU:1, one launch (start us, length us, event | category | flops | bytes accessed | tf_op | source)
XLA Modules:
  0.0 42.9 jit_solution(4992783827422380778)
XLA Ops:
  0.6 40.3 %shard_map.104 = (f32[5,256,128]{2,1,0:T(8,128)}, f32[16,128]{1,0:T(8,128)}) custom-call(f32[5,256,128]{2,1,0:T(8,128)} %bitcast.14, f32[5,256,128]{2,1,0:T(8,128)} %bitcast.15, bf16[75,256,128]{2,1,0:T(8,128)(2,1)} %bitcast.10, bf16[25,256,128]{2,1,0:T(8,128)(2,1)} %bitcast.12, bf16[25,256,128]{2,1,0:T(8,128)(2,1)} %bitcast.13, f32[2,5]{1,0:T(2,128)} %bitcast.18, ...), custom_call_target="tpu_custom_call" | custom-call | tf_op jit(solution)/shard_map/pallas_call | solution.py:482
  41.0 1.9 %shard_map.105 = (f32[5,256,128]{2,1,0:T(8,128)}, f32[16,128]{1,0:T(8,128)}) custom-call(f32[5,256,128]{2,1,0:T(8,128)} %get-tuple-element.6.state_in, f32[16,128]{1,0:T(8,128)} %get-tuple-element.7.patch_in), custom_call_target="tpu_custom_call" | custom-call | tf_op jit(solution)/shard_map/pallas_call | solution.py:544

commit v5 on v4

--- a/solution.py
+++ b/solution.py
@@ -236,6 +236,8 @@
             result.append(psi[u] + step)
         return result
 
+    lax.fori_loop(0, 32, fill, 0)
+
     def n_copy1(d):
         part = pl.ds(4 * d, 4)
         return pltpu.make_async_remote_copy(
@@ -277,7 +279,8 @@
     lax.fori_loop(0, 8, first_part, 0)
     round_wait(0)
     round_start(1)
-    lax.fori_loop(0, 32, fill, 0)
+    loads[4].wait()
+    lax.fori_loop(0, 32, widen, 0)
 
     is_wall = core == sub
     not_wall = jnp.logical_not(is_wall)
@@ -331,8 +334,6 @@
     round_start(2)
     state_copy = pltpu.make_async_copy(psi2, state_h, out_sem)
     state_copy.start()
-    loads[4].wait()
-    lax.fori_loop(0, 32, widen, 0)
 
     def make_contrib(k):
         @pl.when(not_wall)

time: 43 us -> 40.8 us (0.949)
  Pallas kernels: 42.3 us -> 40 us
    pallas_call x1, Pallas kernels: 40.3 us -> 38.1 us  [local(): pl.pallas_call(kernel, out_shape=(jax.ShapeDtypeStruct((NV, 256, 128), F3...]
where the time goes in v5:
time: 40.8 us; the launch traced here: 40.7 us
  Pallas kernels  40 us (98%)
  between operations  0.64 us (2%)
    pallas_call x1, Pallas kernels, local(): pl.pallas_call(kernel, out_shape=(jax.ShapeDtypeStruct((NV, 256, 128), F3...  38.1 us
    pallas_call x1, Pallas kernels, local(): pl.pallas_call(hand_on, out_shape=(jax.ShapeDtypeStruct(state.shape, F32)...  1.94 us

profile of v5, /device:TPU:1, one launch (start us, length us, event | category | flops | bytes accessed | tf_op | source)
XLA Modules:
  0.0 40.7 jit_solution(7100284822334710303)
XLA Ops:
  0.6 38.1 %shard_map.104 = (f32[5,256,128]{2,1,0:T(8,128)}, f32[16,128]{1,0:T(8,128)}) custom-call(f32[5,256,128]{2,1,0:T(8,128)} %bitcast.14, f32[5,256,128]{2,1,0:T(8,128)} %bitcast.15, bf16[75,256,128]{2,1,0:T(8,128)(2,1)} %bitcast.10, bf16[25,256,128]{2,1,0:T(8,128)(2,1)} %bitcast.12, bf16[25,256,128]{2,1,0:T(8,128)(2,1)} %bitcast.13, f32[2,5]{1,0:T(2,128)} %bitcast.18, ...), custom_call_target="tpu_custom_call" | custom-call | tf_op jit(solution)/shard_map/pallas_call | solution.py:483
  38.7 1.9 %shard_map.105 = (f32[5,256,128]{2,1,0:T(8,128)}, f32[16,128]{1,0:T(8,128)}) custom-call(f32[5,256,128]{2,1,0:T(8,128)} %get-tuple-element.6.state_in, f32[16,128]{1,0:T(8,128)} %get-tuple-element.7.patch_in), custom_call_target="tpu_custom_call" | custom-call | tf_op jit(solution)/shard_map/pallas_call | solution.py:545

commit v6 on v5

--- a/solution.py
+++ b/solution.py
@@ -21,7 +21,7 @@
 def kernel(
     start_h, grad_h, jac_h, stab_h, prec_h, weight_h, geom_h, face_h, slot_h,
     state_h, patch_v,
-    psi0, psi1, psi2, grad, jac, stab, prec, geom, weight_s, face_v, slot_v, geom32, onehot, key, contrib, acc,
+    psi0, psi1, psi2, grad, jac, stab, prec, geom, weight_s, face_v, slot_v, geom32, onehot, key, contrib_a, contrib_b, acc,
     nsend0, nrecv0, nsend1, nrecv1, sens_loc, sens,
     core_in, ax_out, ax_in, az_out, az_in, bz_out, bz_in, bx_out, bx_in, y_out, y_in,
     rounds, load_sem, part_sem, out_sem, a_send, a_recv, n0_send, n0_recv, n_send, n_recv, s_send, s_recv,
@@ -336,6 +336,8 @@
     state_copy.start()
 
     def make_contrib(k):
+        contrib = (contrib_a, contrib_b)[k % 2]
+
         @pl.when(not_wall)
         def _():
             s_copy(k).wait_recv()
@@ -344,7 +346,7 @@
         pressure = jnp.transpose(sens[0, part, :])
         shear = jnp.transpose(sens[1, part, :])
         for r in range(8):
-            a = lax.rem(8 * k + 2 + r, 32)
+            a = (8 * k + 2 + r) % 32
             g0 = geom32[a, pl.ds(0, 128, 2), :]
             g1 = geom32[a, pl.ds(1, 128, 2), :]
             c = pressure[:, r:r + 1] * g0 + shear[:, r:r + 1] * g1
@@ -355,18 +357,15 @@
 
     def product(row, rows, k):
         part = onehot[pl.ds(pl.multiple_of(row, 512), rows), pl.ds(pl.multiple_of(k * 1024, 1024), 1024)]
+        contrib = (contrib_a, contrib_b)[k % 2]
         both = jnp.dot(part, contrib[...], preferred_element_type=F32)
         return both[:, 0:128] + both[:, 128:256]
 
-    acc[...] = jnp.zeros((1024, 128), F32)
-
-    def quarter(k, carry):
-        make_contrib(k)
-        acc[...] += product(0, 1024, k)
-        return carry
-
-    lax.fori_loop(0, 3, quarter, 0)
-    make_contrib(3)
+    make_contrib(0)
+    for k in range(3):
+        make_contrib(k + 1)
+        total = product(0, 1024, k)
+        acc[...] = total if k == 0 else acc[...] + total
 
     def c_copy(h):
         return pltpu.make_async_remote_copy(
@@ -500,6 +499,7 @@
             pltpu.VMEM((32, 256, 128), F32),
             pltpu.VMEM((1024, 4096), BF16),
             pltpu.VMEM((32, 128), jnp.int32),
+            pltpu.VMEM((1024, 256), BF16),
             pltpu.VMEM((1024, 256), BF16),
             pltpu.VMEM((1024, 128), F32),
             pltpu.VMEM((NV, 32, 1, 128), F32),

time: 40.8 us -> 40.7 us (level)
  no operation moved by 1% of the time
where the time goes in v6:
time: 40.7 us; the launch traced here: 40.6 us
  Pallas kernels  40 us (98%)
  between operations  0.64 us (2%)
    pallas_call x1, Pallas kernels, local(): pl.pallas_call(kernel, out_shape=(jax.ShapeDtypeStruct((NV, 256, 128), F3...  38 us
    pallas_call x1, Pallas kernels, local(): pl.pallas_call(hand_on, out_shape=(jax.ShapeDtypeStruct(state.shape, F32)...  1.94 us

profile of v6, /device:TPU:1, one launch (start us, length us, event | category | flops | bytes accessed | tf_op | source)
XLA Modules:
  0.0 40.6 jit_solution(3493437448271342392)
XLA Ops:
  0.6 38.0 %shard_map.104 = (f32[5,256,128]{2,1,0:T(8,128)}, f32[16,128]{1,0:T(8,128)}) custom-call(f32[5,256,128]{2,1,0:T(8,128)} %bitcast.14, f32[5,256,128]{2,1,0:T(8,128)} %bitcast.15, bf16[75,256,128]{2,1,0:T(8,128)(2,1)} %bitcast.10, bf16[25,256,128]{2,1,0:T(8,128)(2,1)} %bitcast.12, bf16[25,256,128]{2,1,0:T(8,128)(2,1)} %bitcast.13, f32[2,5]{1,0:T(2,128)} %bitcast.18, ...), custom_call_target="tpu_custom_call" | custom-call | tf_op jit(solution)/shard_map/pallas_call | solution.py:482
  38.7 1.9 %shard_map.105 = (f32[5,256,128]{2,1,0:T(8,128)}, f32[16,128]{1,0:T(8,128)}) custom-call(f32[5,256,128]{2,1,0:T(8,128)} %get-tuple-element.6.state_in, f32[16,128]{1,0:T(8,128)} %get-tuple-element.7.patch_in), custom_call_target="tpu_custom_call" | custom-call | tf_op jit(solution)/shard_map/pallas_call | solution.py:545
